TPU v7x, 32 devices: a whole 2x2x4 slice. The times are simulated.
32 devices in a mesh: section: 4 (over y, x), shard: 2 (over core), tensor: 4 (over z).
Axes of the slice: x: 2, y: 2, z: 4, core: 2. Of those that a mesh axis runs over, the one named last changes fastest.
Arguments:
- grad_terms: float32 [4, 2, 5120, 1280], P('section', 'shard', 'tensor'), may hold values from -5 to 5
- weights: bfloat16 [4, 4, 1280, 1280], P('section', 'tensor', 'shard'), may hold values from -4 to 4
- basis: float32 [4, 1280, 256], P('section'), may hold values from -5 to 5
- first_moment: float32 [4, 4, 1280, 256], P('section', 'tensor', 'shard'), may hold values from -4 to 4
- second_moment: float32 [4, 4, 1280, 256], P('section', 'tensor', 'shard'), may hold values from 0.1 to 2
Outputs:
- new_weights: bfloat16 [4, 4, 1280, 1280], P('section', 'tensor', 'shard')
- new_first: float32 [4, 4, 1280, 256], P('section', 'tensor', 'shard')
- new_second: float32 [4, 4, 1280, 256], P('section', 'tensor', 'shard')
- new_basis: float32 [4, 1280, 256], P('section')
All inputs are finite; a program needn't handle non-finite values.
Results may differ from a plain program's by a relative error of at most 0.001.
Values sent between devices are 32-bit elements; how exact they have to be, the bound alone decides.
A program may use at most 64 MiB of HBM per device.

v0:
```python
import math

import jax
import jax.numpy as jnp
from jax import lax
from jax.sharding import PartitionSpec as P

NS_STEPS = 5


def matmul(left, right):
    return jnp.dot(left, right, precision=lax.Precision.HIGHEST, preferred_element_type=jnp.float32)


def inner_rows(left, right):
    return lax.dot_general(
        left,
        right,
        (((0,), (0,)), ((), ())),
        precision=lax.Precision.HIGHEST,
        preferred_element_type=jnp.float32,
    )


def local_gram(iterate):
    return inner_rows(iterate, iterate)


def newton_steps(power_part, gram_fn):
    gram_now = gram_fn(power_part)
    scaling = lax.rsqrt(jnp.trace(gram_now) + 1e-06)
    iterate = power_part * scaling
    gram_now = gram_now * (scaling * scaling)
    for sweep in range(NS_STEPS):
        iterate = 1.5 * iterate - 0.5 * matmul(iterate, gram_now)
        if sweep + 1 < NS_STEPS:
            gram_now = gram_fn(iterate)
    return iterate


def per_device(grad_terms, weights, basis, first_moment, second_moment):
    gradient = grad_terms[0, 0]
    basis_now = basis[0]
    root_width = math.sqrt(basis_now.shape[0])
    grad_rows = lax.psum_scatter(gradient, "shard", scatter_dimension=0, tiled=True)
    low_rank = matmul(grad_rows, basis_now) / root_width
    power_part = inner_rows(grad_rows, low_rank)
    moment_one = 0.9 * first_moment[0, 0] + 0.1 * low_rank
    moment_two = 0.95 * second_moment[0, 0] + 0.05 * low_rank * low_rank
    direction = moment_one / (jnp.sqrt(moment_two) + 1e-08)
    update = lax.dot_general(
        direction,
        basis_now,
        (((1,), (1,)), ((), ())),
        precision=lax.Precision.HIGHEST,
        preferred_element_type=jnp.float32,
    )
    stepped = weights[0, 0].astype(jnp.float32) - 0.5 * update / root_width
    normed = stepped * lax.rsqrt(jnp.mean(stepped * stepped, axis=1, keepdims=True) + 1e-06)
    new_weights = normed.astype(jnp.bfloat16)
    power = lax.psum(power_part, ("shard", "tensor"))
    iterate = newton_steps(power, local_gram)
    new_basis = iterate * root_width
    return (
        new_weights[None, None],
        moment_one[None, None],
        moment_two[None, None],
        new_basis[None],
    )


def solution(mesh):
    return jax.shard_map(
        per_device,
        mesh=mesh,
        in_specs=(
            P("section", "shard", "tensor", None),
            P("section", "tensor", "shard", None),
            P("section", None, None),
            P("section", "tensor", "shard", None),
            P("section", "tensor", "shard", None),
        ),
        out_specs=(
            P("section", "tensor", "shard", None),
            P("section", "tensor", "shard", None),
            P("section", "tensor", "shard", None),
            P("section", None, None),
        ),
        check_vma=False,
    )
```

profile of v0, /device:TPU:1, one launch (start us, length us, event | category | flops | bytes accessed | tf_op | source)
XLA Modules:
  0.0 121.2 jit_solution(13236282268799067723)
XLA Ops:
  7.2 0.0 copy-start
  7.2 0.0 reduce-scatter.2.cloned.1.call-start
  7.2 0.7 reduce-scatter.2.cloned.1.call-update
  7.9 0.0 all-reduce.2.cloned.1.call-start
  8.0 19.6 %reduce-scatter.2.cloned.1.call-done = f32[640,1280]{1,0:T(8,128)} async-done(((f32[1280,1280]{1,0:T(8,128)}), f32[640,1280]{1,0:T(8,128)}) %reduce-scatter.2.cloned.1.call-update) | async-done | bytes 3276816 | tf_op jit(solution)/shard_map/reduce_scatter | solution.py:45
  27.6 0.0 copy-done
  27.6 0.0 copy-start.1
  27.6 4.8 %fusion.10 = f32[640,256]{1,0:T(8,128)S(1)} fusion(f32[640,1280]{1,0:T(8,128)} %reduce-scatter.2.cloned.1.call-done, f32[1,1280,256]{2,1,0:T(8,128)S(1)} %copy-done), kind=kOutput, calls=%fused_computation.19 | convolution fusion | flops 2516582400 | bytes 5242880 | tf_op jit(solution)/shard_map/dot_general | solution.py:12
  32.4 0.0 copy-done.1
  32.4 4.5 %convolution_bitcast_fusion = f32[1280,256]{0,1:T(8,128)} fusion(f32[640,1280]{1,0:T(8,128)S(1)} %copy-done.1, f32[640,256]{1,0:T(8,128)S(1)} %fusion.10), kind=kOutput, calls=%fused_computation.16 | convolution fusion | flops 2516746240 | bytes 5242880 | tf_op jit(solution)/shard_map/dot_general | solution.py:16
  36.9 0.0 copy-start.3
  36.9 0.0 copy-start.4
  36.9 0.0 all-reduce.2.cloned.1.call-update
  36.9 1.1 copy-done.3
  38.0 0.2 copy-done.4
  38.2 0.0 copy-start.5
  38.2 1.3 %fusion.22 = (f32[1,1,640,256]{3,2,1,0:T(8,128)}, f32[1,1,640,256]{3,2,1,0:T(8,128)}) fusion(f32[640,256]{1,0:T(8,128)S(1)} %fusion.10, f32[1,1,640,256]{3,2,1,0:T(8,128)S(1)} %copy-done.4, f32[1,1,640,256]{3,2,1,0:T(8,128)S(1)} %copy-done.3), kind=kLoop, calls=%fused_computation.35 | loop fusion | flops 1310720 | bytes 3276800 | tf_op jit(solution)/shard_map/broadcast_in_dim | solution.py:67
  39.4 0.6 copy-done.5
  40.1 3.9 %multiply_reduce_fusion = (f32[640]{0:T(1024)S(1)}, f32[640,1280]{1,0:T(8,128)S(1)}) fusion(f32[1,1280,256]{2,1,0:T(8,128)S(1)} %copy-done, f32[640,256]{1,0:T(8,128)S(1)} %fusion.10, f32[1,1,640,256]{3,2,1,0:T(8,128)S(1)} %copy-done.3, f32[1,1,640,256]{3,2,1,0:T(8,128)S(1)} %copy-done.4, bf16[1,1,640,1280]{3,2,1,0:T(8,128)(2,1)S(1)} %copy-done.5), kind=kOutput, calls=%fused_computation.3 | convolution fusion | flops 2522316288 | bytes 8194560 | tf_op jit(solution)/shard_map/dot_general | solution.py:51
  44.0 1.4 %fusion.8 = bf16[1,1,640,1280]{3,2,1,0:T(8,128)(2,1)} fusion(f32[640,1280]{1,0:T(8,128)S(1)} %get-tuple-element.11, f32[640]{0:T(1024)S(1)} %add_rsqrt_fusion), kind=kLoop, calls=%fused_computation.17 | loop fusion | flops 1638400 | bytes 4917760 | tf_op jit(solution)/shard_map/broadcast_in_dim | solution.py:65
  45.4 51.0 %all-reduce.2.cloned.1.call-done = f32[1280,256]{0,1:T(8,128)} async-done(((f32[1280,256]{0,1:T(8,128)}), f32[1280,256]{0,1:T(8,128)}) %all-reduce.2.cloned.1.call-update) | async-done | bytes 1310736 | tf_op jit(solution)/shard_map/psum | solution.py:61
  96.4 0.0 copy-start.2
  96.4 3.7 %select_reduce_fusion = (f32[]{:T(128)}, f32[256,256]{1,0:T(8,128)S(1)}) fusion(f32[1280,256]{0,1:T(8,128)} %all-reduce.2.cloned.1.call-done), kind=kOutput, calls=%fused_computation.32 | convolution fusion | flops 1006829568 | bytes 1572868 | tf_op jit(solution)/shard_map/dot_general | solution.py:16
  100.8 0.0 copy-done.2
  100.8 1.6 %fusion.6 = f32[1280,256]{0,1:T(8,128)S(1)} fusion(f32[1280,256]{0,1:T(8,128)S(1)} %copy-done.2, f32[]{:T(128)S(6)} %rsqrt.12, f32[256,256]{1,0:T(8,128)S(1)} %get-tuple-element.13, f32[]{:T(128)S(6)} %mul.114), kind=kOutput, calls=%fused_computation.14 | convolution fusion | flops 1008336896 | bytes 2883592 | tf_op jit(solution)/shard_map/dot_general | solution.py:12
  102.4 1.2 %fusion.31 = f32[256,256]{1,0:T(8,128)S(1)} fusion(f32[1280,256]{0,1:T(8,128)S(1)} %fusion.6), kind=kOutput, calls=%fused_computation.45 | convolution fusion | flops 1006632960 | bytes 1572864 | tf_op jit(solution)/shard_map/dot_general | solution.py:16
  103.7 1.4 %fusion.5 = f32[1280,256]{0,1:T(8,128)S(1)} fusion(f32[1280,256]{0,1:T(8,128)S(1)} %fusion.6, f32[256,256]{1,0:T(8,128)S(1)} %fusion.31), kind=kOutput, calls=%fused_computation.12 | convolution fusion | flops 1007616000 | bytes 2883584 | tf_op jit(solution)/shard_map/dot_general | solution.py:12
  105.0 1.2 %fusion.32 = f32[256,256]{1,0:T(8,128)S(1)} fusion(f32[1280,256]{0,1:T(8,128)S(1)} %fusion.5), kind=kOutput, calls=%fused_computation.46 | convolution fusion | flops 1006632960 | bytes 1572864 | tf_op jit(solution)/shard_map/dot_general | solution.py:16
  106.3 1.4 %fusion.4 = f32[1280,256]{0,1:T(8,128)S(1)} fusion(f32[1280,256]{0,1:T(8,128)S(1)} %fusion.5, f32[256,256]{1,0:T(8,128)S(1)} %fusion.32), kind=kOutput, calls=%fused_computation.10 | convolution fusion | flops 1007616000 | bytes 2883584 | tf_op jit(solution)/shard_map/dot_general | solution.py:12
  107.6 1.2 %fusion.33 = f32[256,256]{1,0:T(8,128)S(1)} fusion(f32[1280,256]{0,1:T(8,128)S(1)} %fusion.4), kind=kOutput, calls=%fused_computation.47 | convolution fusion | flops 1006632960 | bytes 1572864 | tf_op jit(solution)/shard_map/dot_general | solution.py:16
  108.9 1.4 %fusion.3 = f32[1280,256]{0,1:T(8,128)S(1)} fusion(f32[1280,256]{0,1:T(8,128)S(1)} %fusion.4, f32[256,256]{1,0:T(8,128)S(1)} %fusion.33), kind=kOutput, calls=%fused_computation.8 | convolution fusion | flops 1007616000 | bytes 2883584 | tf_op jit(solution)/shard_map/dot_general | solution.py:12
  110.2 1.2 %fusion.34 = f32[256,256]{1,0:T(8,128)S(1)} fusion(f32[1280,256]{0,1:T(8,128)S(1)} %fusion.3), kind=kOutput, calls=%fused_computation.48 | convolution fusion | flops 1006632960 | bytes 1572864 | tf_op jit(solution)/shard_map/dot_general | solution.py:16
  111.5 1.4 %fusion.7 = f32[1,1280,256]{1,2,0:T(8,128)S(1)} fusion(f32[1280,256]{0,1:T(8,128)S(1)} %fusion.3, f32[256,256]{1,0:T(8,128)S(1)} %fusion.34), kind=kOutput, calls=%fused_computation.15 | convolution fusion | flops 1007943680 | bytes 2883584 | tf_op jit(solution)/shard_map/dot_general | solution.py:12
  112.9 1.5 %copy.14 = f32[1,1280,256]{2,1,0:T(8,128)} copy(f32[1,1280,256]{1,2,0:T(8,128)S(1)} %fusion.7) | data formatting | bytes 2621440
  (1 shorter events, 0.0 us)
Async XLA Ops:
  7.2 20.4 %copy-start = (f32[1,1280,256]{2,1,0:T(8,128)S(1)}, f32[1,1280,256]{2,1,0:T(8,128)}, u32[]{:S(2)}) copy-start(f32[1,1280,256]{2,1,0:T(8,128)} %param.7) | copy-start | bytes 3932164
  7.2 20.4 %reduce-scatter.2.cloned.1.call-start = ((), (), s32[]{:S(2)}) async-start(), calls=%async_computation.1 | async-start | bytes 9830400 | tf_op jit(solution)/shard_map/reduce_scatter | solution.py:45
  7.9 88.4 %all-reduce.2.cloned.1.call-start = ((), (), s32[]{:S(2)}) async-start(), calls=%async_computation.2 | async-start | bytes 2621440 | tf_op jit(solution)/shard_map/psum | solution.py:61
  27.6 4.8 %copy-start.1 = (f32[640,1280]{1,0:T(8,128)S(1)}, f32[640,1280]{1,0:T(8,128)}, u32[]{:S(2)}) copy-start(f32[640,1280]{1,0:T(8,128)} %reduce-scatter.2.cloned.1.call-done) | copy-start | bytes 9830404
  36.9 1.1 copy-start.3
  36.9 1.3 %copy-start.4 = (f32[1,1,640,256]{3,2,1,0:T(8,128)S(1)}, f32[1,1,640,256]{3,2,1,0:T(8,128)}, u32[]{:S(2)}) copy-start(f32[1,1,640,256]{3,2,1,0:T(8,128)} %param.9) | copy-start | bytes 1966084
  38.2 1.9 %copy-start.5 = (bf16[1,1,640,1280]{3,2,1,0:T(8,128)(2,1)S(1)}, bf16[1,1,640,1280]{3,2,1,0:T(8,128)(2,1)}, u32[]{:S(2)}) copy-start(bf16[1,1,640,1280]{3,2,1,0:T(8,128)(2,1)} %param.6) | copy-start | bytes 4915204
  96.4 4.4 %copy-start.2 = (f32[1280,256]{0,1:T(8,128)S(1)}, f32[1280,256]{0,1:T(8,128)}, u32[]{:S(2)}) copy-start(f32[1280,256]{0,1:T(8,128)} %all-reduce.2.cloned.1.call-done) | copy-start | bytes 3932164
Sparse Core Ops, SparseCore 0:
  10.3 17.2 reduce-scatter.1
  37.0 59.2 all-reduce.1
where the time goes:
time: 124 us; the launch traced here: 121 us
  waiting for transfers between devices  71.3 us (58%)
  matrix products  28.9 us (23%)
  between operations  14.8 us (12%)
  local copies, waits for them, and re-layouts  3.37 us (3%)
  other arithmetic  2.69 us (2%)
    psum x1, waiting for transfers between devices, per_device(): power = lax.psum(power_part, ('shard', 'tensor'))  51 us
    reduce_scatter x1, waiting for transfers between devices, per_device(): lax.psum_scatter(gradient, 'shard', scatter_dimension=0, tiled=True)  19.6 us
    dot_general x6, matrix products, inner_rows(): lax.dot_general(left, right, (((0,), (0,)), ((), ())), precision=lax.Prec...  13.2 us
    dot_general x6, matrix products, matmul(): jnp.dot(left, right, precision=lax.Precision.HIGHEST, preferred_element_t...  11.8 us
    dot_general x1, matrix products, per_device(): lax.dot_general(direction, basis_now, (((1,), (1,)), ((), ())), precision...  3.87 us
    unnamed x13, local copies, waits for them, and re-layouts  3.37 us
  transfers between devices with their start and end apart: 2, of which 2 were waited for; matrix products, arithmetic and copies ran while one was open for 5% of the time, Pallas kernels for 0%

commit v1 on v0

v1 whole, which is shorter than its diff:
```python
import functools
import math

import jax
import jax.numpy as jnp
from jax import lax
from jax.experimental import pallas as pl
from jax.experimental.pallas import tpu as pltpu
from jax.sharding import PartitionSpec as P

NS_STEPS = 5
MESH = pl.DeviceIdType.MESH
F32 = jnp.float32
BF16 = jnp.bfloat16
NN = ((1,), (0,))
NT = ((1,), (1,))
TILE = 256
SUBS = 2
SKEW = 2
VMEM_LIMIT = 56 * 1024 * 1024


def split(value):
    high = value.astype(BF16)
    return high, (value - high.astype(F32)).astype(BF16)


def dot3(left, right, dims):
    def one(a, b):
        return lax.dot_general(a, b, (dims, ((), ())), preferred_element_type=F32)

    return one(left[0], right[0]) + (one(left[0], right[1]) + one(left[1], right[0]))


def reduce_kernel(
    n_tensor,
    grad_hbm,
    basis_hbm,
    weight_hbm,
    first_hbm,
    second_hbm,
    weight_out,
    first_out,
    second_out,
    power_out,
    gram_out,
    grad,
    grad_high,
    grad_low,
    basis,
    basis_high,
    basis_low,
    low_mine,
    low_other,
    low_full,
    turned_high,
    turned_low,
    weight,
    first,
    second,
    part,
    part_other,
    own,
    pre_in,
    suf_in,
    pre_out,
    suf_out,
    total,
    in_sem,
    grad_sem,
    low_send,
    low_recv,
    part_send,
    part_recv,
    pre_send,
    pre_recv,
    suf_send,
    suf_recv,
    tot_send,
    tot_recv,
    out_sem,
):
    rows, width = grad.shape
    rank = basis.shape[1]
    half_rows = weight.shape[0]
    half_rank = rank // 2
    sub_rank = half_rank // SUBS
    row_tiles, col_tiles = rows // TILE, width // TILE
    pieces = col_tiles * SUBS
    root_width = math.sqrt(width)
    core = lax.axis_index("shard")
    other = 1 - core
    here = lax.axis_index("tensor")
    has_left, has_right = here > 0, here < n_tensor - 1

    def grad_copy(i):
        at = pl.ds(pl.multiple_of(i * TILE, TILE), TILE)
        return pltpu.make_async_copy(grad_hbm.at[at], grad.at[at], grad_sem.at[i])

    basis_copy = pltpu.make_async_copy(basis_hbm, basis, in_sem.at[0])
    basis_copy.start()
    for i in range(row_tiles):
        grad_copy(i).start()
    state_copies = [
        pltpu.make_async_copy(first_hbm, first, in_sem.at[1]),
        pltpu.make_async_copy(second_hbm, second, in_sem.at[2]),
        pltpu.make_async_copy(weight_hbm, weight, in_sem.at[3]),
    ]
    for copy in state_copies:
        copy.start()

    barrier = pltpu.get_barrier_semaphore()
    pl.semaphore_signal(barrier, inc=1, device_id={"shard": other}, device_id_type=MESH)

    @pl.when(has_left)
    def _():
        pl.semaphore_signal(barrier, inc=1, device_id={"tensor": here - 1}, device_id_type=MESH)

    @pl.when(has_right)
    def _():
        pl.semaphore_signal(barrier, inc=1, device_id={"tensor": here + 1}, device_id_type=MESH)

    basis_copy.wait()
    high, low = split(basis[...])
    basis_high[...] = high
    basis_low[...] = low

    pl.semaphore_wait(barrier, 1 + has_left.astype(jnp.int32) + has_right.astype(jnp.int32))

    def low_copy(i):
        at = pl.ds(pl.multiple_of(i * TILE, TILE), TILE)
        return pltpu.make_async_remote_copy(
            src_ref=low_mine.at[at],
            dst_ref=low_other.at[at],
            send_sem=low_send.at[i],
            recv_sem=low_recv.at[i],
            device_id={"shard": other},
            device_id_type=MESH,
        )

    def project(i, _):
        at = pl.ds(pl.multiple_of(i * TILE, TILE), TILE)
        grad_copy(i).wait()
        pair = split(grad[at, :])
        grad_high[at, :] = pair[0]
        grad_low[at, :] = pair[1]
        low_mine[at, :] = dot3(pair, (basis_high[...], basis_low[...]), NN)
        low_copy(i).start()
        return 0

    lax.fori_loop(0, row_tiles, project, 0)

    def join(i, _):
        at = pl.ds(pl.multiple_of(i * TILE, TILE), TILE)
        low_copy(i).wait_recv()
        block = (low_mine[at, :] + low_other[at, :]) * (1.0 / root_width)
        low_full[at, :] = block
        pair = split(block.T)
        turned_high[:, at] = pair[0]
        turned_low[:, at] = pair[1]
        return 0

    lax.fori_loop(0, row_tiles, join, 0)

    def part_copy(d):
        return pltpu.make_async_remote_copy(
            src_ref=part.at[d, pl.ds(pl.multiple_of(other * half_rank, half_rank), half_rank)],
            dst_ref=part_other.at[d],
            send_sem=part_send.at[d],
            recv_sem=part_recv.at[d],
            device_id={"shard": other},
            device_id_type=MESH,
        )

    def line_copy(source, target, k, send, recv, device):
        return pltpu.make_async_remote_copy(
            src_ref=source.at[k],
            dst_ref=target.at[k],
            send_sem=send.at[k],
            recv_sem=recv.at[k],
            device_id={"tensor": device},
            device_id_type=MESH,
        )

    def pre_copy(source, k):
        return line_copy(source, pre_in, k, pre_send, pre_recv, here + 1)

    def suf_copy(source, k):
        return line_copy(source, suf_in, k, suf_send, suf_recv, here - 1)

    def settle(d):
        part_copy(d).wait_recv()
        for s in range(SUBS):
            k = d * SUBS + s
            mine = pl.ds(pl.multiple_of(core * half_rank + s * sub_rank, sub_rank), sub_rank)
            own[k] = part[d, mine, :] + part_other[d, s * sub_rank : (s + 1) * sub_rank, :]

            @pl.when(jnp.logical_not(has_left))
            def _():
                pre_copy(own, k).start()

            @pl.when(jnp.logical_not(has_right))
            def _():
                suf_copy(own, k).start()

    def power_tile(d, _):
        at = pl.ds(pl.multiple_of(d * TILE, TILE), TILE)
        part[d] = dot3(
            (turned_high[...], turned_low[...]), (grad_high[:, at], grad_low[:, at]), NN
        )
        part_copy(d).start()

        @pl.when(d >= 1)
        def _():
            settle(d - 1)

        return 0

    lax.fori_loop(0, col_tiles, power_tile, 0)
    settle(col_tiles - 1)
    for copy in state_copies:
        copy.wait()

    def forward_pre(k):
        @pl.when(has_left)
        def _():
            pre_copy(pre_out, k).wait_recv()

            @pl.when(has_right)
            def _():
                pre_out[k] = pre_in[k] + own[k]
                pre_copy(pre_out, k).start()

    def forward_suf(k):
        @pl.when(has_right)
        def _():
            suf_copy(suf_out, k).wait_recv()

            @pl.when(has_left)
            def _():
                suf_out[k] = suf_in[k] + own[k]
                suf_copy(suf_out, k).start()

    def total_copy(k):
        d, s = k // SUBS, k % SUBS
        at = pl.ds(pl.multiple_of(core * half_rank + s * sub_rank, sub_rank), sub_rank)
        return pltpu.make_async_remote_copy(
            src_ref=total.at[d, at],
            dst_ref=total.at[d, at],
            send_sem=tot_send.at[k],
            recv_sem=tot_recv.at[k],
            device_id={"shard": other},
            device_id_type=MESH,
        )

    def finish(k):
        d, s = k // SUBS, k % SUBS
        at = pl.ds(pl.multiple_of(core * half_rank + s * sub_rank, sub_rank), sub_rank)

        @pl.when(jnp.logical_not(has_left))
        def _():
            total[d, at, :] = own[k] + suf_in[k]

        @pl.when(jnp.logical_not(has_right))
        def _():
            total[d, at, :] = own[k] + pre_in[k]

        @pl.when(jnp.logical_and(has_left, has_right))
        def _():
            total[d, at, :] = own[k] + (pre_in[k] + suf_in[k])

        total_copy(k).start()

    step_rows = half_rows // col_tiles

    def state_copy_out(source, target, j, which):
        at = pl.ds(pl.multiple_of(j * step_rows, 16), step_rows)
        return pltpu.make_async_copy(source.at[at], target.at[at], out_sem.at[which, j])

    def out_copies(j):
        return [
            state_copy_out(weight, weight_out, j, 0),
            state_copy_out(first, first_out, j, 1),
            state_copy_out(second, second_out, j, 2),
        ]

    def update_rows(j):
        at = pl.ds(pl.multiple_of(j * step_rows, 16), step_rows)
        low_rank = low_full[pl.ds(pl.multiple_of(core * half_rows + j * step_rows, 16), step_rows), :]
        moment_one = 0.9 * first[at, :] + 0.1 * low_rank
        moment_two = 0.95 * second[at, :] + 0.05 * low_rank * low_rank
        first[at, :] = moment_one
        second[at, :] = moment_two
        direction = moment_one / (jnp.sqrt(moment_two) + 1e-08)
        update = dot3(split(direction), (basis_high[...], basis_low[...]), NT)
        stepped = weight[at, :].astype(F32) - (0.5 / root_width) * update
        mean = jnp.mean(stepped * stepped, axis=1, keepdims=True)
        weight[at, :] = (stepped * lax.rsqrt(mean + 1e-06)).astype(BF16)
        for copy in out_copies(j):
            copy.start()

    gram_out[...] = jnp.zeros_like(gram_out)

    def gram_tile(d):
        for s in range(SUBS):
            total_copy(d * SUBS + s).wait_recv()
        block = total[d]
        pair = split(block)
        gram_out[...] += dot3(pair, pair, NT)
        power_out[pl.ds(pl.multiple_of(d * TILE, TILE), TILE), :] = block.T

    left_side = 2 * here < n_tensor

    def line_step(step, _):
        @pl.when(step < pieces)
        def _():
            @pl.when(left_side)
            def _():
                forward_pre(step)

            @pl.when(jnp.logical_not(left_side))
            def _():
                forward_suf(step)

        @pl.when(step >= SKEW)
        def _():
            k = step - SKEW

            @pl.when(left_side)
            def _():
                forward_suf(k)

            @pl.when(jnp.logical_not(left_side))
            def _():
                forward_pre(k)

            finish(k)

            @pl.when(jnp.logical_and(k % SUBS == SUBS - 1, k >= 2 * SUBS - 1))
            def _():
                gram_tile(k // SUBS - 1)

        @pl.when(jnp.logical_and(step % SUBS == 0, step < pieces))
        def _():
            update_rows(step // SUBS)

        return 0

    lax.fori_loop(0, pieces + SKEW, line_step, 0)
    gram_tile(col_tiles - 1)

    def drain(d, _):
        low_copy(d).wait_send()
        part_copy(d).wait_send()
        for copy in out_copies(d):
            copy.wait()
        for s in range(SUBS):
            k = d * SUBS + s
            total_copy(k).wait_send()

            @pl.when(has_right)
            def _():
                pre_copy(pre_out, k).wait_send()

            @pl.when(has_left)
            def _():
                suf_copy(suf_out, k).wait_send()

        return 0

    lax.fori_loop(0, col_tiles, drain, 0)


def newton_scale(gram, dot):
    size = gram.shape[0]
    rows = lax.broadcasted_iota(jnp.int32, (size, size), 0)
    columns = lax.broadcasted_iota(jnp.int32, (size, size), 1)
    eye = jnp.where(rows == columns, 1.0, 0.0).astype(F32)
    scaling = lax.rsqrt(jnp.sum(gram * eye) + 1e-06)
    now = gram * (scaling * scaling)
    product = None
    for sweep in range(NS_STEPS):
        factor = 1.5 * eye - 0.5 * now
        if sweep + 1 < NS_STEPS:
            now = dot(dot(now, factor), factor)
        product = factor if product is None else dot(product, factor)
    return product, scaling


def finish_kernel(
    power_ref, gram_ref, weight_in, first_in, second_in,
    weight_out, first_out, second_out, basis_out, sem,
):
    copies = [
        pltpu.make_async_copy(weight_in, weight_out, sem.at[0]),
        pltpu.make_async_copy(first_in, first_out, sem.at[1]),
        pltpu.make_async_copy(second_in, second_out, sem.at[2]),
    ]
    for copy in copies:
        copy.start()
    product, scaling = newton_scale(
        gram_ref[...], lambda a, b: dot3(split(a), split(b), NN)
    )
    product = split(product * (scaling * math.sqrt(power_ref.shape[0])))
    for d in range(power_ref.shape[0] // TILE):
        at = pl.ds(d * TILE, TILE)
        basis_out[at, :] = dot3(split(power_ref[at, :]), product, NN)
    for copy in copies:
        copy.wait()


def fused_device(n_tensor, grad_terms, weights, basis, first_moment, second_moment):
    rows, width = grad_terms.shape[2:]
    rank = basis.shape[2]
    half_rows = rows // 2
    tiles = width // TILE
    row_tiles = rows // TILE
    pieces = tiles * SUBS
    piece = (pieces, rank // 2 // SUBS, TILE)
    hbm = pl.BlockSpec(memory_space=pl.ANY)
    vmem = pl.BlockSpec(memory_space=pltpu.VMEM)
    dma = pltpu.SemaphoreType.DMA
    state = [
        jax.ShapeDtypeStruct((half_rows, width), BF16),
        jax.ShapeDtypeStruct((half_rows, rank), F32),
        jax.ShapeDtypeStruct((half_rows, rank), F32),
    ]
    new_weights, new_first, new_second, power, gram = pl.pallas_call(
        functools.partial(reduce_kernel, n_tensor),
        out_shape=state
        + [
            jax.ShapeDtypeStruct((width, rank), F32),
            jax.ShapeDtypeStruct((rank, rank), F32),
        ],
        in_specs=[hbm] * 5,
        out_specs=[hbm, hbm, hbm, vmem, vmem],
        scratch_shapes=[
            pltpu.VMEM((rows, width), F32),
            pltpu.VMEM((rows, width), BF16),
            pltpu.VMEM((rows, width), BF16),
            pltpu.VMEM((width, rank), F32),
            pltpu.VMEM((width, rank), BF16),
            pltpu.VMEM((width, rank), BF16),
            pltpu.VMEM((rows, rank), F32),
            pltpu.VMEM((rows, rank), F32),
            pltpu.VMEM((rows, rank), F32),
            pltpu.VMEM((rank, rows), BF16),
            pltpu.VMEM((rank, rows), BF16),
            pltpu.VMEM((half_rows, width), BF16),
            pltpu.VMEM((half_rows, rank), F32),
            pltpu.VMEM((half_rows, rank), F32),
            pltpu.VMEM((tiles, rank, TILE), F32),
            pltpu.VMEM((tiles, rank // 2, TILE), F32),
            pltpu.VMEM(piece, F32),
            pltpu.VMEM(piece, F32),
            pltpu.VMEM(piece, F32),
            pltpu.VMEM(piece, F32),
            pltpu.VMEM(piece, F32),
            pltpu.VMEM((tiles, rank, TILE), F32),
            dma((4,)),
            dma((row_tiles,)),
            dma((row_tiles,)),
            dma((row_tiles,)),
            dma((tiles,)),
            dma((tiles,)),
            dma((pieces,)),
            dma((pieces,)),
            dma((pieces,)),
            dma((pieces,)),
            dma((pieces,)),
            dma((pieces,)),
            dma((3, tiles)),
        ],
        compiler_params=pltpu.CompilerParams(
            collective_id=0, has_side_effects=True, vmem_limit_bytes=VMEM_LIMIT
        ),
        name="reduce",
    )(grad_terms[0, 0], basis[0], weights[0, 0], first_moment[0, 0], second_moment[0, 0])
    new_weights, new_first, new_second, new_basis = pl.pallas_call(
        finish_kernel,
        out_shape=state + [jax.ShapeDtypeStruct((width, rank), F32)],
        in_specs=[vmem, vmem, hbm, hbm, hbm],
        out_specs=[hbm, hbm, hbm, vmem],
        scratch_shapes=[dma((3,))],
        compiler_params=pltpu.CompilerParams(vmem_limit_bytes=VMEM_LIMIT),
        name="finish",
    )(power, gram, new_weights, new_first, new_second)
    return (
        new_weights[None, None],
        new_first[None, None],
        new_second[None, None],
        new_basis[None],
    )


def dot_high(left, right, dims=NN):
    return lax.dot_general(
        left, right, (dims, ((), ())), precision=lax.Precision.HIGH, preferred_element_type=F32
    )


def plain_device(grad_terms, weights, basis, first_moment, second_moment):
    basis_now = basis[0]
    root_width = math.sqrt(basis_now.shape[0])
    grad_rows = lax.psum_scatter(grad_terms[0, 0], "shard", scatter_dimension=0, tiled=True)
    low_rank = dot_high(grad_rows, basis_now) / root_width
    power_part = dot_high(grad_rows, low_rank, ((0,), (0,)))
    power = lax.psum(power_part, ("shard", "tensor"))
    moment_one = 0.9 * first_moment[0, 0] + 0.1 * low_rank
    moment_two = 0.95 * second_moment[0, 0] + 0.05 * low_rank * low_rank
    direction = moment_one / (jnp.sqrt(moment_two) + 1e-08)
    update = dot_high(direction, basis_now, NT)
    stepped = weights[0, 0].astype(F32) - 0.5 * update / root_width
    normed = stepped * lax.rsqrt(jnp.mean(stepped * stepped, axis=1, keepdims=True) + 1e-06)
    product, scaling = newton_scale(dot_high(power, power, ((0,), (0,))), dot_high)
    new_basis = dot_high(power, product) * (scaling * root_width)
    return (
        normed.astype(BF16)[None, None],
        moment_one[None, None],
        moment_two[None, None],
        new_basis[None],
    )


def solution(mesh):
    n_shard, n_tensor = mesh.shape["shard"], mesh.shape["tensor"]

    def per_device(grad_terms, weights, basis, first_moment, second_moment):
        args = (grad_terms, weights, basis, first_moment, second_moment)
        if n_shard == 2 and n_tensor > 1:
            return fused_device(n_tensor, *args)
        return plain_device(*args)

    return jax.shard_map(
        per_device,
        mesh=mesh,
        in_specs=(
            P("section", "shard", "tensor", None),
            P("section", "tensor", "shard", None),
            P("section", None, None),
            P("section", "tensor", "shard", None),
            P("section", "tensor", "shard", None),
        ),
        out_specs=(
            P("section", "tensor", "shard", None),
            P("section", "tensor", "shard", None),
            P("section", "tensor", "shard", None),
            P("section", None, None),
        ),
        check_vma=False,
    )
```

time: 124 us -> 133 us (1.073); the launches traced: 121 us -> 132 us
  Pallas kernels: 0 us -> 132 us
  waiting for transfers between devices: 71.3 us -> 0 us
  matrix products: 28.9 us -> 0 us
  between operations: 14.8 us -> 0.64 us
  local copies, waits for them, and re-layouts: 3.37 us -> 0 us
  other arithmetic: 2.69 us -> 0 us
    pallas_call x0 -> x2, Pallas kernels: none -> 132 us  [the longest x1 92.9 us: fused_device(): pl.pallas_call(finish_kernel, out_shape=state + [jax.ShapeDtypeStruct((wi...]
    psum x1 -> x0, waiting for transfers between devices: 51 us -> none  [per_device(): power = lax.psum(power_part, ('shard', 'tensor'))]
    dot_general x13 -> x0, matrix products: 28.9 us -> none  [the longest x6 13.2 us: inner_rows(): lax.dot_general(left, right, (((0,), (0,)), ((), ())), precision=lax.Prec...]
    reduce_scatter x1 -> x0, waiting for transfers between devices: 19.6 us -> none  [per_device(): lax.psum_scatter(gradient, 'shard', scatter_dimension=0, tiled=True)]
    unnamed x13 -> x0, local copies, waits for them, and re-layouts: 3.37 us -> none
    broadcast_in_dim x2 -> x0, other arithmetic: 2.68 us -> none  [the longest x1 1.41 us: per_device(): new_weights[None, None]]
  transfers between devices with their start and end apart: 2 -> 0, of which waited for: 2 -> 0; matrix products, arithmetic and copies ran while one was open for 5% -> 0% of each run, Pallas kernels for 0% -> 0%
where the time goes in v1:
time: 133 us; the launch traced here: 132 us
  Pallas kernels  132 us (99%)
    pallas_call x1, Pallas kernels, fused_device(): pl.pallas_call(finish_kernel, out_shape=state + [jax.ShapeDtypeStruct((wi...  92.9 us
    pallas_call x1, Pallas kernels, fused_device(): pl.pallas_call(functools.partial(reduce_kernel, n_tensor), out_shape=stat...  38.9 us

profile of v1, /device:TPU:1, one launch (start us, length us, event | category | flops | bytes accessed | tf_op | source)
XLA Modules:
  0.0 132.4 jit_solution(7628008407729171583)
XLA Ops:
  0.6 38.9 %reduce.1 = (bf16[640,1280]{1,0:T(8,128)(2,1)}, f32[640,256]{1,0:T(8,128)}, f32[640,256]{1,0:T(8,128)}, f32[1280,256]{1,0:T(8,128)}, f32[256,256]{1,0:T(8,128)}) custom-call(f32[1280,1280]{1,0:T(8,128)} %bitcast.9, f32[1280,256]{1,0:T(8,128)} %bitcast.11, bf16[640,1280]{1,0:T(8,128)(2,1)} %bitcast.10, f32[640,256]{1,0:T(8,128)} %bitcast.12, f32[640,256]{1,0:T(8,128)} %bitcast.13), custom_call_target="tpu_custom_call" | custom-call | tf_op jit(solution)/shard_map/reduce/pallas_call | solution.py:428
  39.5 92.9 %finish.1 = (bf16[640,1280]{1,0:T(8,128)(2,1)}, f32[640,256]{1,0:T(8,128)}, f32[640,256]{1,0:T(8,128)}, f32[1280,256]{1,0:T(8,128)}) custom-call(f32[1280,256]{1,0:T(8,128)} %get-tuple-element.13.power_ref, f32[256,256]{1,0:T(8,128)} %get-tuple-element.14.gram_ref, bf16[640,1280]{1,0:T(8,128)(2,1)} %get-tuple-element.15.weight_in, ...), custom_call_target="tpu_custom_call" | custom-call | tf_op jit(solution)/shard_map/finish/pallas_call | solution.py:479

commit v2 on v1

--- a/solution.py
+++ b/solution.py
@@ -16,7 +16,7 @@
 NT = ((1,), (1,))
 TILE = 256
 SUBS = 2
-SKEW = 2
+SKEW = 3
 VMEM_LIMIT = 56 * 1024 * 1024
 
 
@@ -371,7 +371,7 @@
     lax.fori_loop(0, col_tiles, drain, 0)
 
 
-def newton_scale(gram, dot):
+def newton_scale(gram, dot, between=None):
     size = gram.shape[0]
     rows = lax.broadcasted_iota(jnp.int32, (size, size), 0)
     columns = lax.broadcasted_iota(jnp.int32, (size, size), 1)
@@ -381,6 +381,8 @@
     product = None
     for sweep in range(NS_STEPS):
         factor = 1.5 * eye - 0.5 * now
+        if sweep == 2 and between is not None:
+            between()
         if sweep + 1 < NS_STEPS:
             now = dot(dot(now, factor), factor)
         product = factor if product is None else dot(product, factor)
@@ -389,23 +391,27 @@
 
 def finish_kernel(
     power_ref, gram_ref, weight_in, first_in, second_in,
-    weight_out, first_out, second_out, basis_out, sem,
+    weight_out, first_out, second_out, basis_out, weight, first, second, in_sem, out_sem,
 ):
-    copies = [
-        pltpu.make_async_copy(weight_in, weight_out, sem.at[0]),
-        pltpu.make_async_copy(first_in, first_out, sem.at[1]),
-        pltpu.make_async_copy(second_in, second_out, sem.at[2]),
-    ]
-    for copy in copies:
+    held = ((weight_in, weight, weight_out), (first_in, first, first_out), (second_in, second, second_out))
+    loads = [pltpu.make_async_copy(a, b, in_sem.at[i]) for i, (a, b, _) in enumerate(held)]
+    stores = [pltpu.make_async_copy(b, c, out_sem.at[i]) for i, (_, b, c) in enumerate(held)]
+    for copy in loads:
         copy.start()
+
+    def pass_on():
+        for load, store in zip(loads, stores):
+            load.wait()
+            store.start()
+
     product, scaling = newton_scale(
-        gram_ref[...], lambda a, b: dot3(split(a), split(b), NN)
+        gram_ref[...], lambda a, b: dot3(split(a), split(b), NN), pass_on
     )
     product = split(product * (scaling * math.sqrt(power_ref.shape[0])))
     for d in range(power_ref.shape[0] // TILE):
         at = pl.ds(d * TILE, TILE)
         basis_out[at, :] = dot3(split(power_ref[at, :]), product, NN)
-    for copy in copies:
+    for copy in stores:
         copy.wait()
 
 
@@ -481,7 +487,13 @@
         out_shape=state + [jax.ShapeDtypeStruct((width, rank), F32)],
         in_specs=[vmem, vmem, hbm, hbm, hbm],
         out_specs=[hbm, hbm, hbm, vmem],
-        scratch_shapes=[dma((3,))],
+        scratch_shapes=[
+            pltpu.VMEM((half_rows, width), BF16),
+            pltpu.VMEM((half_rows, rank), F32),
+            pltpu.VMEM((half_rows, rank), F32),
+            dma((3,)),
+            dma((3,)),
+        ],
         compiler_params=pltpu.CompilerParams(vmem_limit_bytes=VMEM_LIMIT),
         name="finish",
     )(power, gram, new_weights, new_first, new_second)

time: 133 us -> 45.2 us (0.34)
  Pallas kernels: 132 us -> 44.4 us
    pallas_call x1, Pallas kernels: 92.9 us -> 6.52 us  [fused_device(): pl.pallas_call(finish_kernel, out_shape=state + [jax.ShapeDtypeStruct((wi...]
where the time goes in v2:
time: 45.2 us; the launch traced here: 45 us
  Pallas kernels  44.4 us (98%)
  between operations  0.64 us (1%)
    pallas_call x1, Pallas kernels, fused_device(): pl.pallas_call(functools.partial(reduce_kernel, n_tensor), out_shape=stat...  37.8 us
    pallas_call x1, Pallas kernels, fused_device(): pl.pallas_call(finish_kernel, out_shape=state + [jax.ShapeDtypeStruct((wi...  6.52 us

profile of v2, /device:TPU:1, one launch (start us, length us, event | category | flops | bytes accessed | tf_op | source)
XLA Modules:
  0.0 45.0 jit_solution(16062499503097981054)
XLA Ops:
  0.6 37.8 %reduce.1 = (bf16[640,1280]{1,0:T(8,128)(2,1)}, f32[640,256]{1,0:T(8,128)}, f32[640,256]{1,0:T(8,128)}, f32[1280,256]{1,0:T(8,128)}, f32[256,256]{1,0:T(8,128)}) custom-call(f32[1280,1280]{1,0:T(8,128)} %bitcast.9, f32[1280,256]{1,0:T(8,128)} %bitcast.11, bf16[640,1280]{1,0:T(8,128)(2,1)} %bitcast.10, f32[640,256]{1,0:T(8,128)} %bitcast.12, f32[640,256]{1,0:T(8,128)} %bitcast.13), custom_call_target="tpu_custom_call" | custom-call | tf_op jit(solution)/shard_map/reduce/pallas_call | solution.py:434
  38.5 6.5 %finish.1 = (bf16[640,1280]{1,0:T(8,128)(2,1)}, f32[640,256]{1,0:T(8,128)}, f32[640,256]{1,0:T(8,128)}, f32[1280,256]{1,0:T(8,128)}) custom-call(f32[1280,256]{1,0:T(8,128)} %get-tuple-element.13.power_ref, f32[256,256]{1,0:T(8,128)} %get-tuple-element.14.gram_ref, bf16[640,1280]{1,0:T(8,128)(2,1)} %get-tuple-element.15.weight_in, ...), custom_call_target="tpu_custom_call" | custom-call | tf_op jit(solution)/shard_map/finish/pallas_call | solution.py:485
